TPU v7x, 512 devices: a whole 4x8x8 slice. The times are simulated.
512 devices in a mesh: grp: 32 (over y, z_hi, core), leaf: 16 (over z_lo, x).
Axes of the slice: x: 4, y: 8, z: 8 (z_hi: 2, z_lo: 4; z = z_hi * 4 + z_lo), core: 2. Of those that a mesh axis runs over, the one named last changes fastest.
Arguments:
- vectors: bfloat16 [32, 2097152], P(None, ('grp', 'leaf')), may hold values from -6 to 6
- offsets: bfloat16 [3, 2097152], P(None, ('grp', 'leaf')), may hold values from 0 to 1
- near_list: int32 [8192, 16], P(('grp', 'leaf')), may hold values from 0 to 8191, as said below
- near_count: int32 [8192], P(('grp', 'leaf')), may hold values from 8 to 16, as said below
- leaf_basis: bfloat16 [8192, 64, 256], P(('grp', 'leaf')), may hold values from -0.375 to 0.375
- far_list: int32 [8192, 16], P(('grp', 'leaf')), may hold values from 0 to 8191, as said below
- far_count: int32 [8192], P(('grp', 'leaf')), may hold values from 0 to 16, as said below
- leaf_coupling: bfloat16 [8192, 16, 64, 64], P(('grp', 'leaf')), as said below
- transfer: bfloat16 [8192, 64, 64], P(('grp', 'leaf')), may hold values from -0.75 to 0.75
- group_list: int32 [32, 16], P('grp'), may hold values from 0 to 31, as said below
- group_count: int32 [32], P('grp'), may hold values from 8 to 16, as said below
- group_coupling: bfloat16 [32, 16, 64, 64], P('grp', 'leaf'), may hold values from -0.01171875 to 0.01171875
Outputs:
- applied: bfloat16 [32, 2097152], P(None, ('grp', 'leaf'))
Inputs may be any that keep to these rules, and one draw needn't show every extreme that they name: `near_list`: the first near_count[l] entries of row l are distinct leaves of l's own group lying on l's device or on the devices just before and after it along leaf (16 consecutive leaves a device); the first entry is l itself and the remaining entries repeat l. `near_count`: the first leaf of every device has exactly 16. `far_list`: the first far_count[l] entries of row l are distinct leaves of l's own group other than l; the remaining entries repeat l. If leaf j stands in slot k < far_count[l] of row l, then l stands in some slot k2 < far_count[j] of row j. `far_count`: the first leaf of every group has exactly 16. If far_list[l, k] = j with k < far_count[l], and far_list[j, k2] = l with k2 < far_count[j], then leaf_coupling[j, k2] is the transpose of leaf_coupling[l, k]. `group_list`: the first group_count[g] entries of row g are distinct groups other than g; the remaining entries repeat g. `group_count`: group 0 has exactly 16.
All inputs are finite; a program needn't handle non-finite values.
Results may differ from a plain program's by a relative error of at most 0.005.
Values may be sent and summed in bfloat16 or wider, within the bound.
No kernel may reach another device: no remote copies, remote signals or barrier semaphores. Data moves between devices by JAX's collectives and lax.ppermute only.
A program may use at most 64 MiB of HBM per device.

v0:
```python
import jax
import jax.numpy as jnp
from jax import lax
from jax.sharding import PartitionSpec as P

inv_four_pi = 0.07957747154594767
soften = 0.01


def with_halo(shard, sides, width):
    for axis, dim in sides:
        count, length = (lax.axis_size(axis), shard.shape[dim])
        up = [(i, (i + 1) % count) for i in range(count - 1)]
        down = [(j, i) for i, j in up]
        last = lax.slice_in_dim(shard, length - width, length, axis=dim)
        first = lax.slice_in_dim(shard, 0, width, axis=dim)
        before = lax.ppermute(last, axis, up)
        after = lax.ppermute(first, axis, down)
        shard = jnp.concatenate([before, shard, after], axis=dim)
    return shard


def centres(leaf_ids):
    columns = []
    for axis_pos in range(3):
        summed = jnp.zeros_like(leaf_ids)
        for bit_pos in range(10):
            picked = jnp.bitwise_and(jnp.right_shift(leaf_ids, 3 * bit_pos + axis_pos), 1)
            summed = summed + jnp.left_shift(picked, bit_pos)
        columns.append(summed.astype(jnp.float32))
    return jnp.stack(columns)


def kernel_tile(source_pts, target_pts):
    squared = jnp.zeros(
        (source_pts.shape[0], source_pts.shape[2], target_pts.shape[1]), jnp.float32
    )
    for axis_pos in range(3):
        spacing = source_pts[:, axis_pos, :, None] - target_pts[axis_pos][None, None, :]
        squared = squared + spacing * spacing
    return inv_four_pi * lax.rsqrt(squared + soften)


def body(
    vectors,
    offsets,
    near_list,
    near_count,
    leaf_basis,
    far_list,
    far_count,
    leaf_coupling,
    transfer,
    group_list,
    group_count,
    group_coupling,
):
    leaf_devices = lax.axis_size("leaf")
    local_leaves = near_list.shape[0]
    near_slots = near_list.shape[1]
    far_slots = far_list.shape[1]
    vec_count = vectors.shape[0]
    leaf_width = vectors.shape[1] // local_leaves
    group_leaves = leaf_devices * local_leaves
    leaf_place = lax.axis_index("leaf")
    group_place = lax.axis_index("grp")
    device_first = (group_place * leaf_devices + leaf_place) * local_leaves
    group_first = group_place * group_leaves
    window_first = device_first - local_leaves
    stacked = jnp.concatenate([vectors, offsets], axis=0)
    widened = with_halo(stacked, (("leaf", 1),), local_leaves * leaf_width)
    window_vectors = widened[:vec_count].reshape(vec_count, 3 * local_leaves, leaf_width)
    window_ids = window_first + jnp.arange(3 * local_leaves, dtype=jnp.int32)
    window_pts = (
        widened[vec_count:].astype(jnp.float32).reshape(3, 3 * local_leaves, leaf_width)
        + centres(window_ids)[:, :, None]
    )
    slot_ids = jnp.arange(near_slots, dtype=jnp.int32)

    def near_step(running, target):
        sources = near_list[target] - window_first
        active_slots = slot_ids < near_count[target]
        source_pts = jnp.take(window_pts, sources, axis=1).transpose(1, 0, 2)
        target_pts = lax.dynamic_index_in_dim(window_pts, local_leaves + target, 1, keepdims=False)
        near_tile = jnp.where(
            active_slots[:, None, None], kernel_tile(source_pts, target_pts), 0.0
        ).astype(jnp.bfloat16)
        source_vectors = jnp.take(window_vectors, sources, axis=1)
        return (
            running,
            jnp.einsum(
                "vkb,kba->va", source_vectors, near_tile, preferred_element_type=jnp.float32
            ),
        )

    ignored, near_field = lax.scan(near_step, 0, jnp.arange(local_leaves, dtype=jnp.int32))
    leaf_vectors = vectors.reshape(vec_count, local_leaves, leaf_width)
    coeffs = jnp.einsum(
        "via,ira->ivr", leaf_vectors, leaf_basis, preferred_element_type=jnp.float32
    ).astype(jnp.bfloat16)
    far_active = jnp.arange(far_slots, dtype=jnp.int32)[None, :] < far_count[:, None]
    far_rows = far_list - group_first
    group_coeffs = lax.all_gather(coeffs, "leaf", axis=0, tiled=True)
    picked = jnp.take(group_coeffs, far_rows, axis=0)
    picked = jnp.where(far_active[:, :, None, None], picked, jnp.zeros((), jnp.bfloat16))
    far_field = jnp.einsum(
        "ikvs,ikrs->ivr", picked, leaf_coupling, preferred_element_type=jnp.float32
    )
    coarse_part = jnp.einsum("ivs,isr->vr", coeffs, transfer, preferred_element_type=jnp.float32)
    coarse = lax.psum(coarse_part, "leaf").astype(jnp.bfloat16)
    all_coarse = lax.all_gather(coarse[None], "grp", axis=0, tiled=True)
    group_active = jnp.arange(group_list.shape[1], dtype=jnp.int32) < group_count[0]
    own_slots = group_coupling.shape[1]
    slot_first = leaf_place * own_slots
    own_groups = lax.dynamic_slice_in_dim(group_list[0], slot_first, own_slots, 0)
    own_active = lax.dynamic_slice_in_dim(group_active, slot_first, own_slots, 0)
    picked_groups = jnp.where(
        own_active[:, None, None],
        jnp.take(all_coarse, own_groups, axis=0),
        jnp.zeros((), jnp.bfloat16),
    )
    coarse_term = jnp.einsum(
        "kvs,krs->vr", picked_groups, group_coupling[0], preferred_element_type=jnp.float32
    )
    coarse_out = lax.psum(coarse_term, "leaf")
    downward = jnp.einsum(
        "vs,irs->ivr", coarse_out.astype(jnp.bfloat16), transfer, preferred_element_type=jnp.float32
    )
    local_coeffs = (far_field + downward).astype(jnp.bfloat16)
    expanded = jnp.einsum(
        "ivr,ira->via", local_coeffs, leaf_basis, preferred_element_type=jnp.float32
    )
    result = jnp.transpose(near_field, (1, 0, 2)) + expanded
    return result.reshape(vec_count, local_leaves * leaf_width).astype(jnp.bfloat16)


def solution(mesh):
    placed = (
        P(None, ("grp", "leaf")),
        P(None, ("grp", "leaf")),
        P(("grp", "leaf"), None),
        P(("grp", "leaf")),
        P(("grp", "leaf"), None, None),
        P(("grp", "leaf"), None),
        P(("grp", "leaf")),
        P(("grp", "leaf"), None, None, None),
        P(("grp", "leaf"), None, None),
        P("grp", None),
        P("grp"),
        P("grp", "leaf", None, None),
    )
    return jax.shard_map(
        body, mesh=mesh, in_specs=placed, out_specs=P(None, ("grp", "leaf")), check_vma=False
    )
```

profile of v0, /device:TPU:8, one launch (start us, length us, event | category | flops | bytes accessed | tf_op | source)
XLA Modules:
  0.0 398.0 jit_solution(17522042291182980777)
XLA Ops:
  9.7 4.6 %collective-permute-start = (bf16[35,4096]{1,0:T(8,128)(2,1)S(1)}, bf16[35,4096]{1,0:T(8,128)(2,1)S(1)}, u32[]{:S(2)}, u32[]{:S(2)}) collective-permute-start(bf16[35,4096]{1,0:T(8,128)(2,1)S(1)} %constant_dynamic-update-slice_fusion), channel_id=1, source_target_pairs={{0,1},{1,2},{2,3},{3,4},{4,5},{5,6},{6,7},{7,8},{8,9},{9,10},{10,1... | collective-permute-start | bytes 860168 | tf_op jit(solution)/shard_map/ppermute | solution.py:17
  14.3 1.9 convolution_convert_fusion
  22.5 80.5 %psum.14 = bf16[32,64]{1,0:T(8,128)(2,1)S(1)} all-reduce(f32[32,64]{1,0:T(8,128)S(1)} %convolution_bitcast_fusion.1), channel_id=1, replica_groups=mesh['grp'=32,'leaf'=16] {'leaf'}, use_global_device_ids=true, to_apply=%region_2.3 | all-reduce | flops 2048 | bytes 12288 | tf_op jit(solution)/shard_map/psum | solution.py:110
  103.0 53.7 %all-gather = bf16[1024,64]{1,0:T(8,128)(2,1)S(1)} all-gather(bf16[32,64]{1,0:T(8,128)(2,1)S(1)} %psum.14), channel_id=2, replica_groups=mesh['grp'=32,'leaf'=16] {'grp'}, dimensions={0}, use_global_device_ids=true | all-gather | bytes 135168 | tf_op jit(solution)/shard_map/all_gather | solution.py:111
  158.2 74.2 %psum.15 = bf16[32,64]{1,0:T(8,128)(2,1)S(1)} all-reduce(f32[32,64]{1,0:T(8,128)S(1)} %fusion.30), channel_id=1, replica_groups=mesh['grp'=32,'leaf'=16] {'leaf'}, use_global_device_ids=true, to_apply=%region_3.4 | all-reduce | flops 2048 | bytes 12288 | tf_op jit(solution)/shard_map/psum | solution.py:125
  233.6 148.9 %while.15 = (s32[]{:T(128)}, f32[16,32,256]{2,1,0:T(8,128)S(1)}, s32[16]{0:T(128)S(1)}, s32[16,16]{1,0:T(8,128)}, s32[]{:T(128)}, /*index=5*/bf16[32,48,256]{2,0...) while((s32[]{:T(128)}, f32[16,32,256]{2,1,0:T(8,128)S(1)}, ...), condition=%wide.region_1.2_spmd.clone, body=%wide.region_0.1_spmd.clone.sunk | while | flops 79836360 | bytes 1276693 | solution.py:96
  241.1 1.9 fusion.62
  250.4 1.9 fusion.62
  259.7 1.9 fusion.62
  269.0 1.9 fusion.62
  278.3 1.9 fusion.62
  287.6 1.9 fusion.62
  296.9 1.9 fusion.62
  306.2 1.9 fusion.62
  315.6 1.9 fusion.62
  324.9 1.9 fusion.62
  334.2 1.9 fusion.62
  343.5 1.9 fusion.62
  352.8 1.9 fusion.62
  362.1 1.9 fusion.62
  371.4 1.9 fusion.62
  380.7 1.9 fusion.62
  382.6 2.6 gather_fusion.2
  385.2 3.8 fusion.20
  (244 shorter events, 86.8 us)
Async XLA Ops:
  6.5 7.7 %copy-start = (bf16[16,64,256]{2,1,0:T(8,128)(2,1)S(1)}, bf16[16,64,256]{2,1,0:T(8,128)(2,1)}, u32[]{:S(2)}) copy-start(bf16[16,64,256]{2,1,0:T(8,128)(2,1)} %param.18) | copy-start | bytes 1572868
  6.5 376.0 %all-gather.3.cloned.1.call-start = ((), (), s32[]{:S(2)}) async-start(), calls=%async_computation | async-start | bytes 2228224 | tf_op jit(solution)/shard_map/all_gather | solution.py:103
  8.4 224.9 %collective-permute-start.1 = (bf16[35,4096]{1,0:T(8,128)(2,1)S(1)}, bf16[35,4096]{1,0:T(8,128)(2,1)S(1)}, u32[]{:S(2)}, u32[]{:S(2)}) collective-permute-start(bf16[35,4096]{1,0:T(8,128)(2,1)S(1)} %constant_dynamic-update-slice_fusion), channel_id=1, source_target_pairs={{1,0},{2,1},{3,2},{4,3},{5,4},{6,5},{7,6},{8,7},{9,8},{10,9},{11,1... | collective-permute-start | bytes 860168 | tf_op jit(solution)/shard_map/ppermute | solution.py:18
  9.7 223.6 %collective-permute-start = (bf16[35,4096]{1,0:T(8,128)(2,1)S(1)}, bf16[35,4096]{1,0:T(8,128)(2,1)S(1)}, u32[]{:S(2)}, u32[]{:S(2)}) collective-permute-start(bf16[35,4096]{1,0:T(8,128)(2,1)S(1)} %constant_dynamic-update-slice_fusion), channel_id=1, source_target_pairs={{0,1},{1,2},{2,3},{3,4},{4,5},{5,6},{6,7},{7,8},{8,9},{9,10},{10,1... | collective-permute-start | bytes 860168 | tf_op jit(solution)/shard_map/ppermute | solution.py:17
  14.2 219.4 %copy-start.2 = (s32[16]{0:T(128)S(1)}, s32[16]{0:T(128)}, u32[]{:S(2)}) copy-start(s32[16]{0:T(128)} %param.17) | copy-start | bytes 196
  385.2 3.8 copy-start.1
Sparse Core Ops, SparseCore 0:
  16.3 92.5 all-gather.2
where the time goes:
time: 400 us; the launch traced here: 398 us
  blocking collectives  208 us (52%)
  local copies, waits for them, and re-layouts  47.7 us (12%)
  loops' own time  44.3 us (11%)
  matrix products  39.6 us (10%)
  other arithmetic  36.2 us (9%)
  between operations  15.9 us (4%)
  starting transfers between devices  5.86 us (1%)
    psum x1, blocking collectives, body(): coarse = lax.psum(coarse_part, 'leaf').astype(jnp.bfloat16)  80.5 us
    psum x1, blocking collectives, body(): coarse_out = lax.psum(coarse_term, 'leaf')  74.2 us
    all_gather x1, blocking collectives, body(): all_coarse = lax.all_gather(coarse[None], 'grp', axis=0, tiled=True)  53.7 us
    another operation x1, loops' own time, body(): lax.scan(near_step, 0, jnp.arange(local_leaves, dtype=jnp.int32))  44.3 us
    dot_general x16, matrix products, near_step(): jnp.einsum('vkb,kba->va', source_vectors, near_tile, preferred_element_ty...  29.8 us
    and x16, other arithmetic, near_step(): source_vectors = jnp.take(window_vectors, sources, axis=1)  21.9 us
    select_n x16, other arithmetic, near_step(): source_vectors = jnp.take(window_vectors, sources, axis=1)  11.1 us
    dynamic_slice x16, local copies, waits for them, and re-layouts, body(): lax.scan(near_step, 0, jnp.arange(local_leaves, dtype=jnp.int32))  10.5 us
  transfers between devices with their start and end apart: 3, of which 0 were waited for; matrix products, arithmetic and copies ran while one was open for 28% of the time, Pallas kernels for 0%

commit v1 on v0

--- a/solution.py
+++ b/solution.py
@@ -122,7 +122,7 @@
     coarse_term = jnp.einsum(
         "kvs,krs->vr", picked_groups, group_coupling[0], preferred_element_type=jnp.float32
     )
-    coarse_out = lax.psum(coarse_term, "leaf")
+    coarse_out = jnp.sum(jax.lax.all_gather(coarse_term, "leaf"), axis=0)
     downward = jnp.einsum(
         "vs,irs->ivr", coarse_out.astype(jnp.bfloat16), transfer, preferred_element_type=jnp.float32
     )

time: 400 us -> 367 us (0.917)
  the two profiles are of different devices: /device:TPU:8 before, /device:TPU:2 now
where the time goes in v1:
time: 367 us; the launch traced here: 365 us
  blocking collectives  171 us (47%)
  local copies, waits for them, and re-layouts  47.7 us (13%)
  loops' own time  44.3 us (12%)
  matrix products  39.7 us (11%)
  other arithmetic  36.3 us (10%)
  between operations  15.9 us (4%)
  starting transfers between devices  9.74 us (3%)
    psum x1, blocking collectives, body(): coarse = lax.psum(coarse_part, 'leaf').astype(jnp.bfloat16)  72.3 us
    all_gather x1, blocking collectives, body(): all_coarse = lax.all_gather(coarse[None], 'grp', axis=0, tiled=True)  54.6 us
    all_gather x1, blocking collectives, body(): coarse_out = jnp.sum(jax.lax.all_gather(coarse_term, 'leaf'), axis=0)  44.3 us
    another operation x1, loops' own time, body(): lax.scan(near_step, 0, jnp.arange(local_leaves, dtype=jnp.int32))  44.3 us
    dot_general x16, matrix products, near_step(): jnp.einsum('vkb,kba->va', source_vectors, near_tile, preferred_element_ty...  29.8 us
    and x16, other arithmetic, near_step(): source_vectors = jnp.take(window_vectors, sources, axis=1)  22 us
    select_n x16, other arithmetic, near_step(): source_vectors = jnp.take(window_vectors, sources, axis=1)  11.1 us
    dynamic_slice x16, local copies, waits for them, and re-layouts, body(): lax.scan(near_step, 0, jnp.arange(local_leaves, dtype=jnp.int32))  10.5 us
  transfers between devices with their start and end apart: 3, of which 0 were waited for; matrix products, arithmetic and copies ran while one was open for 31% of the time, Pallas kernels for 0%

profile of v1, /device:TPU:2, one launch (start us, length us, event | category | flops | bytes accessed | tf_op | source)
XLA Modules:
  0.0 364.7 jit_solution(16499446873418673432)
XLA Ops:
  8.4 7.8 %collective-permute-start.1 = (bf16[35,4096]{1,0:T(8,128)(2,1)S(1)}, bf16[35,4096]{1,0:T(8,128)(2,1)S(1)}, u32[]{:S(2)}, u32[]{:S(2)}) collective-permute-start(bf16[35,4096]{1,0:T(8,128)(2,1)S(1)} %constant_dynamic-update-slice_fusion), channel_id=1, source_target_pairs={{1,0},{2,1},{3,2},{4,3},{5,4},{6,5},{7,6},{8,7},{9,8},{10,9},{11,1... | collective-permute-start | bytes 860168 | tf_op jit(solution)/shard_map/ppermute | solution.py:18
  16.2 1.9 collective-permute-start
  18.1 1.9 convolution_convert_fusion
  26.4 72.3 %psum.7 = bf16[32,64]{1,0:T(8,128)(2,1)S(1)} all-reduce(f32[32,64]{1,0:T(8,128)S(1)} %convolution_bitcast_fusion.1), channel_id=1, replica_groups=mesh['grp'=32,'leaf'=16] {'leaf'}, use_global_device_ids=true, to_apply=%region_2.3 | all-reduce | flops 2048 | bytes 12288 | tf_op jit(solution)/shard_map/psum | solution.py:110
  98.7 54.6 %all-gather = bf16[1024,64]{1,0:T(8,128)(2,1)S(1)} all-gather(bf16[32,64]{1,0:T(8,128)(2,1)S(1)} %psum.7), channel_id=2, replica_groups=mesh['grp'=32,'leaf'=16] {'grp'}, dimensions={0}, use_global_device_ids=true | all-gather | bytes 135168 | tf_op jit(solution)/shard_map/all_gather | solution.py:111
  154.8 44.3 %all-gather.1 = f32[512,64]{1,0:T(8,128)S(1)} all-gather(f32[32,64]{1,0:T(8,128)S(1)} %fusion.30), channel_id=3, replica_groups=mesh['grp'=32,'leaf'=16] {'leaf'}, dimensions={0}, use_global_device_ids=true | all-gather | bytes 139264 | tf_op jit(solution)/shard_map/all_gather | solution.py:125
  200.3 148.9 %while.15 = (s32[]{:T(128)}, f32[16,32,256]{2,1,0:T(8,128)S(1)}, s32[16]{0:T(128)S(1)}, s32[16,16]{1,0:T(8,128)}, s32[]{:T(128)}, /*index=5*/bf16[32,48,256]{2,0...) while((s32[]{:T(128)}, f32[16,32,256]{2,1,0:T(8,128)S(1)}, ...), condition=%wide.region_1.2_spmd.clone, body=%wide.region_0.1_spmd.clone.sunk | while | flops 79836360 | bytes 1276693 | solution.py:96
  207.8 1.9 fusion.62
  217.1 1.9 fusion.62
  226.4 1.9 fusion.62
  235.7 1.9 fusion.62
  245.0 1.9 fusion.62
  254.3 1.9 fusion.62
  263.6 1.9 fusion.62
  272.9 1.9 fusion.62
  282.2 1.9 fusion.62
  291.5 1.9 fusion.62
  300.8 1.9 fusion.62
  310.1 1.9 fusion.62
  319.4 1.9 fusion.62
  328.8 1.9 fusion.62
  338.1 1.9 fusion.62
  349.2 2.6 gather_fusion.2
  351.8 3.8 %fusion.20 = f32[16,32,64]{2,1,0:T(8,128)} fusion(bf16[16,16,64,64]{3,2,1,0:T(8,128)(2,1)} %param.21, bf16[16,16,32,64]{3,2,1,0:T(8,128)(2,1)S(1)} %bitcast.108, pred[16,16]{1,0:T(8,128)(4,1)S(1)} %get-tuple-element.195, pred[16,16]{1,0:T(8,128)(4,1)S(1)} %iota_compare_fusion), kind=kOutput, calls=%fused_computation.38 | convolution fusion | flops 68157440 | bytes 3277312 | tf_op jit(solution)/shard_map/ikvs,ikrs->ivr/dot_general | solution.py:106
  (245 shorter events, 87.4 us)
Async XLA Ops:
  6.5 11.6 %copy-start = (bf16[16,64,256]{2,1,0:T(8,128)(2,1)S(1)}, bf16[16,64,256]{2,1,0:T(8,128)(2,1)}, u32[]{:S(2)}) copy-start(bf16[16,64,256]{2,1,0:T(8,128)(2,1)} %param.18) | copy-start | bytes 1572868
  6.5 342.7 %all-gather.4.cloned.1.call-start = ((), (), s32[]{:S(2)}) async-start(), calls=%async_computation | async-start | bytes 2228224 | tf_op jit(solution)/shard_map/all_gather | solution.py:103
  8.4 191.5 %collective-permute-start.1 = (bf16[35,4096]{1,0:T(8,128)(2,1)S(1)}, bf16[35,4096]{1,0:T(8,128)(2,1)S(1)}, u32[]{:S(2)}, u32[]{:S(2)}) collective-permute-start(bf16[35,4096]{1,0:T(8,128)(2,1)S(1)} %constant_dynamic-update-slice_fusion), channel_id=1, source_target_pairs={{1,0},{2,1},{3,2},{4,3},{5,4},{6,5},{7,6},{8,7},{9,8},{10,9},{11,1... | collective-permute-start | bytes 860168 | tf_op jit(solution)/shard_map/ppermute | solution.py:18
  16.2 183.7 %collective-permute-start = (bf16[35,4096]{1,0:T(8,128)(2,1)S(1)}, bf16[35,4096]{1,0:T(8,128)(2,1)S(1)}, u32[]{:S(2)}, u32[]{:S(2)}) collective-permute-start(bf16[35,4096]{1,0:T(8,128)(2,1)S(1)} %constant_dynamic-update-slice_fusion), channel_id=1, source_target_pairs={{0,1},{1,2},{2,3},{3,4},{4,5},{5,6},{6,7},{7,8},{8,9},{9,10},{10,1... | collective-permute-start | bytes 860168 | tf_op jit(solution)/shard_map/ppermute | solution.py:17
  20.0 180.3 %copy-start.2 = (s32[16]{0:T(128)S(1)}, s32[16]{0:T(128)}, u32[]{:S(2)}) copy-start(s32[16]{0:T(128)} %param.17) | copy-start | bytes 196
  351.8 3.8 %copy-start.1 = (bf16[16,64,64]{2,1,0:T(8,128)(2,1)S(1)}, bf16[16,64,64]{2,1,0:T(8,128)(2,1)}, u32[]{:S(2)}) copy-start(bf16[16,64,64]{2,1,0:T(8,128)(2,1)} %param.22) | copy-start | bytes 393220
Sparse Core Ops, SparseCore 0:
  20.1 88.4 all-gather.3
